TPU v7x, 256 devices: a whole 4x4x8 slice. The times are simulated.
256 devices in a mesh: copy: 64 (over z_hi, y, x), tp: 4 (over z_lo, core).
Axes of the slice: x: 4, y: 4, z: 8 (z_hi: 4, z_lo: 2; z = z_hi * 2 + z_lo), core: 2. Of those that a mesh axis runs over, the one named last changes fastest.
Arguments:
- layer_inputs: bfloat16 [64, 6, 512, 4, 1024], P('copy', None, None, 'tp'), may hold values from -16 to 16
- output_grads: bfloat16 [64, 6, 512, 1024], P('copy', None, 'tp'), may hold values from -6 to 6
- value_weights: bfloat16 [64, 4, 1024, 1024], P('copy', 'tp'), may hold values from -16 to 16
Outputs:
- merged: bfloat16 [4, 1024, 1024], P('tp', 'copy')
- fisher_mean: float32 [4, 1024, 1024], P('tp', 'copy')
All inputs are finite; a program needn't handle non-finite values.
Results may differ from a plain program's by a relative error of at most 0.001.
Values may be sent and summed in bfloat16 or wider, within the bound.
A program may use at most 128 MiB of HBM per device.

v0:
```python
import jax
import jax.numpy as jnp
from jax import lax
from jax.sharding import PartitionSpec as P

epsilon = 1e-06


def local(layer_inputs, output_grads, value_weights):
    batches = layer_inputs.shape[1]
    tokens = layer_inputs.shape[2]
    features = layer_inputs.shape[4]
    columns = output_grads.shape[3]
    own_weights = value_weights[0]
    zero_grid = jnp.zeros((features, columns), jnp.float32)
    fisher = zero_grid
    for batch_index in range(batches):
        inputs_mb = layer_inputs[0, batch_index, :, 0, :]

        def add_rows(carried, shard_rows, first_row, inputs_mb=inputs_mb):
            product = lax.dot_general(
                inputs_mb, shard_rows, (((0,), (0,)), ((), ())), preferred_element_type=jnp.float32
            )
            return product

        gradient = add_rows(
            zero_grid,
            lax.all_gather(output_grads[0, batch_index], "tp", axis=0, tiled=True),
            jnp.int32(0),
        )
        fisher = fisher + gradient * gradient
    fisher = (fisher / (batches * tokens))[None]
    weighted = fisher * own_weights.astype(jnp.float32)
    summed_weighted, summed_fisher = (
        lax.psum_scatter(weighted, "copy", scatter_dimension=1, tiled=True),
        lax.psum_scatter(fisher, "copy", scatter_dimension=1, tiled=True),
    )
    copies = lax.axis_size("copy")
    fisher_mean = summed_fisher / copies
    merged = (summed_weighted / (summed_fisher + epsilon)).astype(jnp.bfloat16)
    return (merged, fisher_mean)


def solution(mesh):
    return jax.shard_map(
        local,
        mesh=mesh,
        in_specs=(
            P("copy", None, None, "tp", None),
            P("copy", None, "tp", None),
            P("copy", "tp", None, None),
        ),
        out_specs=(P("tp", "copy", None), P("tp", "copy", None)),
        check_vma=False,
    )
```

profile of v0, /device:TPU:0, one launch (start us, length us, event | category | flops | bytes accessed | tf_op | source)
XLA Modules:
  0.0 966.9 jit_solution(7915721599127481844)
XLA Ops:
  7.2 0.0 all-gather.15.cloned.1.call-start
  7.2 2.5 fusion.24
  9.8 0.0 all-gather.15.cloned.1.call-update
  9.8 0.0 all-gather.13.cloned.1.call-start
  9.8 0.7 all-gather.13.cloned.1.call-update
  10.5 0.0 all-gather.21.cloned.1.call-start
  10.6 0.7 all-gather.21.cloned.1.call-update
  11.3 0.0 all-gather.19.cloned.1.call-start
  11.3 0.5 all-gather.19.cloned.1.call-update
  11.8 0.0 all-gather.17.cloned.1.call-start
  11.9 0.5 all-gather.17.cloned.1.call-update
  12.4 0.0 all-gather.23.cloned.1.call-start
  12.5 0.5 all-gather.23.cloned.1.call-update
  13.0 0.0 reduce-scatter.3.cloned.1.call-start
  13.1 21.4 %all-gather.15.cloned.1.call-done = bf16[1,1,512,1024]{3,2,1,0:T(8,128)(2,1)} async-done(((bf16[1,1,128,1024]{3,2,1,0:T(8,128)(2,1)}), bf16[1,1,512,1024]{3,2,1,0:T(8,128)(2,1)}) %all-gather.15.cloned.1.call-update) | async-done | bytes 1048592 | tf_op jit(solution)/shard_map/all_gather | solution.py:28
  34.5 4.8 fusion.12
  39.2 21.2 %all-gather.13.cloned.1.call-done = bf16[1,1,512,1024]{3,2,1,0:T(8,128)(2,1)} async-done(((bf16[1,1,128,1024]{3,2,1,0:T(8,128)(2,1)}), bf16[1,1,512,1024]{3,2,1,0:T(8,128)(2,1)}) %all-gather.13.cloned.1.call-update) | async-done | bytes 1048592 | tf_op jit(solution)/shard_map/all_gather | solution.py:28
  60.4 4.8 fusion.15
  65.3 21.1 %all-gather.21.cloned.1.call-done = bf16[1,1,512,1024]{3,2,1,0:T(8,128)(2,1)} async-done(((bf16[1,1,128,1024]{3,2,1,0:T(8,128)(2,1)}), bf16[1,1,512,1024]{3,2,1,0:T(8,128)(2,1)}) %all-gather.21.cloned.1.call-update) | async-done | bytes 1048592 | tf_op jit(solution)/shard_map/all_gather | solution.py:28
  86.4 4.8 fusion.3
  91.2 21.0 %all-gather.19.cloned.1.call-done = bf16[1,1,512,1024]{3,2,1,0:T(8,128)(2,1)} async-done(((bf16[1,1,128,1024]{3,2,1,0:T(8,128)(2,1)}), bf16[1,1,512,1024]{3,2,1,0:T(8,128)(2,1)}) %all-gather.19.cloned.1.call-update) | async-done | bytes 1048592 | tf_op jit(solution)/shard_map/all_gather | solution.py:28
  112.2 4.8 fusion.6
  117.0 21.0 %all-gather.17.cloned.1.call-done = bf16[1,1,512,1024]{3,2,1,0:T(8,128)(2,1)} async-done(((bf16[1,1,128,1024]{3,2,1,0:T(8,128)(2,1)}), bf16[1,1,512,1024]{3,2,1,0:T(8,128)(2,1)}) %all-gather.17.cloned.1.call-update) | async-done | bytes 1048592 | tf_op jit(solution)/shard_map/all_gather | solution.py:28
  138.0 4.8 fusion.9
  142.8 0.0 copy-start.1
  142.8 21.0 %all-gather.23.cloned.1.call-done = bf16[1,1,512,1024]{3,2,1,0:T(8,128)(2,1)} async-done(((bf16[1,1,128,1024]{3,2,1,0:T(8,128)(2,1)}), bf16[1,1,512,1024]{3,2,1,0:T(8,128)(2,1)}) %all-gather.23.cloned.1.call-update) | async-done | bytes 1048592 | tf_op jit(solution)/shard_map/all_gather | solution.py:28
  163.8 10.1 %add_multiply_fusion = f32[1024,1024]{1,0:T(8,128)S(1)} fusion(f32[1024,1024]{1,0:T(8,128)} %fusion.3, f32[1024,1024]{1,0:T(8,128)} %fusion.6, f32[1024,1024]{1,0:T(8,128)} %fusion.9, f32[1024,1024]{1,0:T(8,128)} %fusion.12, f32[1024,1024]{1,0:T(8,128)} %fusion.15, bf16[1,1,512,1024]{3,2,1,0:T(8,128)(2,1)} %all-gather.23.cloned.1.call-done, ...), kind=kOutput, calls=%fused_computation.2 | convolution fusion | flops 1086324736 | bytes 27262976 | tf_op jit(solution)/shard_map/dot_general | solution.py:21
  173.9 0.0 copy-start
  173.9 1.9 copy-done
  175.8 0.0 copy-done.1
  175.8 3.1 fusion
  178.9 0.0 reduce-scatter.3.cloned.1.call-update
  178.9 0.0 reduce-scatter.5.cloned.1.call-start
  179.0 0.7 reduce-scatter.5.cloned.1.call-update
  179.7 391.2 %reduce-scatter.3.cloned.1.call-done = f32[1,16,1024]{2,1,0:T(8,128)} async-done(((f32[1,1024,1024]{2,1,0:T(8,128)}), f32[1,16,1024]{2,1,0:T(8,128)}) %reduce-scatter.3.cloned.1.call-update) | async-done | bytes 65552 | tf_op jit(solution)/shard_map/reduce_scatter | solution.py:35
  570.9 387.6 %reduce-scatter.5.cloned.1.call-done = f32[1,16,1024]{2,1,0:T(8,128)} async-done(((f32[1,1024,1024]{2,1,0:T(8,128)}), f32[1,16,1024]{2,1,0:T(8,128)}) %reduce-scatter.5.cloned.1.call-update) | async-done | bytes 65552 | tf_op jit(solution)/shard_map/reduce_scatter | solution.py:36
  958.5 1.5 broadcast_multiply_fusion
Async XLA Ops:
  7.2 27.3 %all-gather.15.cloned.1.call-start = ((), (), s32[]{:S(2)}) async-start(), calls=%async_computation.5 | async-start | bytes 1310720 | tf_op jit(solution)/shard_map/all_gather | solution.py:28
  9.8 50.6 %all-gather.13.cloned.1.call-start = ((), (), s32[]{:S(2)}) async-start(), calls=%async_computation.4 | async-start | bytes 1310720 | tf_op jit(solution)/shard_map/all_gather | solution.py:28
  10.5 75.9 %all-gather.21.cloned.1.call-start = ((), (), s32[]{:S(2)}) async-start(), calls=%async_computation.8 | async-start | bytes 1310720 | tf_op jit(solution)/shard_map/all_gather | solution.py:28
  11.3 100.9 %all-gather.19.cloned.1.call-start = ((), (), s32[]{:S(2)}) async-start(), calls=%async_computation.7 | async-start | bytes 1310720 | tf_op jit(solution)/shard_map/all_gather | solution.py:28
  11.8 126.1 %all-gather.17.cloned.1.call-start = ((), (), s32[]{:S(2)}) async-start(), calls=%async_computation.6 | async-start | bytes 1310720 | tf_op jit(solution)/shard_map/all_gather | solution.py:28
  12.4 151.4 %all-gather.23.cloned.1.call-start = ((), (), s32[]{:S(2)}) async-start(), calls=%async_computation.9 | async-start | bytes 1310720 | tf_op jit(solution)/shard_map/all_gather | solution.py:28
  13.0 557.9 %reduce-scatter.3.cloned.1.call-start = ((), (), s32[]{:S(2)}) async-start(), calls=%async_computation.2 | async-start | bytes 4259840 | tf_op jit(solution)/shard_map/reduce_scatter | solution.py:35
  142.8 33.1 %copy-start.1 = (bf16[1,1,1024,1024]{3,2,1,0:T(8,128)(2,1)S(1)}, bf16[1,1,1024,1024]{3,2,1,0:T(8,128)(2,1)}, u32[]{:S(2)}) copy-start(bf16[1,1,1024,1024]{3,2,1,0:T(8,128)(2,1)} %param.5) | copy-start | bytes 6291460
  173.9 1.9 copy-start
  178.9 779.6 %reduce-scatter.5.cloned.1.call-start = ((), (), s32[]{:S(2)}) async-start(), calls=%async_computation.3 | async-start | bytes 4259840 | tf_op jit(solution)/shard_map/reduce_scatter | solution.py:36
Sparse Core Ops, SparseCore 0:
  9.9 24.5 all-gather.14
  36.3 24.0 all-gather.12
  62.2 24.0 all-gather.20
  88.0 24.0 all-gather.18
  113.8 24.0 all-gather.16
  139.7 24.0 all-gather.22
  179.0 391.8 reduce-scatter.2
  573.6 384.8 reduce-scatter.4
where the time goes:
time: 967 us
  waiting for transfers between devices  909 us (94%)
  matrix products  34 us (4%)
  between operations  14.2 us (1%)
    reduce_scatter x1, waiting for transfers between devices, local(): lax.psum_scatter(weighted, 'copy', scatter_dimension=1, tiled=True)  391 us
    reduce_scatter x1, waiting for transfers between devices, local(): lax.psum_scatter(fisher, 'copy', scatter_dimension=1, tiled=True)  388 us
    all_gather x6, waiting for transfers between devices, local(): lax.all_gather(output_grads[0, batch_index], 'tp', axis=0, tiled=True)  127 us
    dot_general x6, matrix products, add_rows(): lax.dot_general(inputs_mb, shard_rows, (((0,), (0,)), ((), ())), preferre...  34 us
  transfers between devices with their start and end apart: 8, of which 8 were waited for; matrix products, arithmetic and copies ran while one was open for 2% of the time, Pallas kernels for 0%

commit v1 on v0

v1 whole, which is shorter than its diff:
```python
import jax
import jax.numpy as jnp
from jax import lax
from jax.experimental import pallas as pl
from jax.experimental.pallas import tpu as pltpu
from jax.sharding import PartitionSpec as P

EPSILON = 1e-6
RING = 4
HALF = RING // 2
ROWS = 16
CW = 128
LAG1, LAG2, LAG3 = 2, 3, 4
MESH = pl.DeviceIdType.MESH


def kernel(x_hbm, g_hbm, w_hbm, merged_ref, mean_ref,
           xv, xt, g, wv, f, rwx, rwy, r1x, r1y, s2x, s2y, r2x, r2y, s3, r3,
           x_sem, g_sem, w_sem, send_sem, rz, rc, rr, rw, r1_sem, r2_sem, r3_sem):
    batches, tokens, features = x_hbm.shape
    own_tokens = g_hbm.shape[1]
    blocks = g.shape[0]
    copy, tp = lax.axis_index("copy"), lax.axis_index("tp")
    z, y, x = copy // 16, (copy // 4) % 4, copy % 4
    chip, core = tp // 2, tp % 2

    def turn(v, by):
        return lax.rem(v + by, RING)

    def at(zz, yy, xx):
        return (zz * 16 + yy * 4 + xx, tp)

    pair = (copy, (1 - chip) * 2 + core)
    sibling = (copy, chip * 2 + 1 - core)
    own_rows = pl.ds(pl.multiple_of(tp * own_tokens, own_tokens), own_tokens)
    pair_rows = pl.ds(pl.multiple_of(pair[1] * own_tokens, own_tokens), own_tokens)

    loads = []
    for k in range(blocks):
        loads.append(pltpu.make_async_copy(
            g_hbm.at[:, :, pl.ds(k * CW, CW)], g.at[k, :, own_rows, :], g_sem.at[k]))
    w_load = pltpu.make_async_copy(w_hbm, wv, w_sem)
    x_loads = [pltpu.make_async_copy(x_hbm.at[m], xv.at[m], x_sem.at[m]) for m in range(batches)]
    for load in loads:
        load.start()
    w_load.start()
    for load in x_loads:
        load.start()

    barrier = pltpu.get_barrier_semaphore()
    partners = [pair, sibling]
    for d in range(1, RING):
        partners += [at(z, y, turn(x, d)), at(z, turn(y, d), x), at(turn(z, d), y, x)]
    for partner in partners:
        pl.semaphore_signal(barrier, 1, device_id=partner, device_id_type=MESH)
    pl.semaphore_wait(barrier, len(partners))

    def send(src, dst, slot, recv, to):
        pltpu.make_async_remote_copy(src, dst, send_sem.at[slot], recv, device_id=to, device_id_type=MESH).start()

    def take(ref, sem):
        pltpu.make_async_copy(ref, ref, sem).wait()

    for k in range(blocks):
        loads[k].wait()
        own = g.at[k, :, own_rows, :]
        send(own, own, 0, rz.at[k], pair)
        send(own, own, 1, rc.at[k], sibling)
    w_load.wait()
    for d in range(1, RING):
        send(wv.at[pl.ds(0, HALF), :, turn(x, d)], rwx.at[d - 1], 3, rw.at[0], at(z, y, turn(x, d)))
        send(wv.at[pl.ds(HALF, HALF), turn(y, d)], rwy.at[d - 1], 3, rw.at[1], at(z, turn(y, d), x))

    for m in range(batches):
        x_loads[m].wait()

        def turn_tile(i, c, m=m):
            cols = pl.ds(pl.multiple_of(i * 256, 256), 256)
            xt[m, cols, :] = xv[m, :, cols].T
            return c

        lax.fori_loop(0, features // 256, turn_tile, 0)

    def relay(k):
        got = g.at[k, :, pair_rows, :]
        take(got, rz.at[k])
        send(got, got, 2, rr.at[k], sibling)

    def compute(k):
        got = g.at[k, :, own_rows, :]
        take(got, rc.at[k])
        take(got, rr.at[k])

        def tile(i, c):
            rows = pl.ds(pl.multiple_of(i * 256, 256), 256)
            total = None
            for m in range(batches):
                gradient = jnp.dot(xt[m, rows, :], g[k, m], preferred_element_type=jnp.float32)
                square = gradient * gradient
                total = square if total is None else total + square
            f[k, i] = total.reshape(RING, RING, ROWS, CW)
            return c

        lax.fori_loop(0, HALF, tile, 0)
        for d in range(1, RING):
            send(f.at[k, pl.ds(0, HALF), :, turn(x, d)], r1x.at[k, d - 1], 4, r1_sem.at[0, k],
                 at(z, y, turn(x, d)))
        lax.fori_loop(HALF, RING, tile, 0)
        for d in range(1, RING):
            send(f.at[k, pl.ds(HALF, HALF), turn(y, d)], r1y.at[k, d - 1], 5, r1_sem.at[1, k],
                 at(z, turn(y, d), x))

    def stage1(k):
        cols = pl.ds(pl.multiple_of(k * CW, CW), CW)

        def add(own_f, own_w, rf, rw_):
            fisher = own_f
            weighted = own_f * own_w.astype(jnp.float32)
            for d in range(RING - 1):
                fisher = fisher + rf[k, d]
                weighted = weighted + rf[k, d] * rw_[d, :, :, :, cols].astype(jnp.float32)
            return weighted, fisher

        take(r1x.at[k], r1_sem.at[0, k])
        weighted, fisher = add(f[k, pl.ds(0, HALF), :, x], wv[pl.ds(0, HALF), :, x, :, cols], r1x, rwx)
        s2x[k, :, 0] = weighted
        s2x[k, :, 1] = fisher
        for d in range(1, RING):
            send(s2x.at[k, :, :, turn(y, d)], r2x.at[k, d - 1], 6, r2_sem.at[0, k], at(z, turn(y, d), x))
        take(r1y.at[k], r1_sem.at[1, k])
        weighted, fisher = add(f[k, pl.ds(HALF, HALF), y], wv[pl.ds(HALF, HALF), y, :, :, cols], r1y, rwy)
        s2y[k, :, 0] = weighted
        s2y[k, :, 1] = fisher
        for d in range(1, RING):
            send(s2y.at[k, :, :, turn(x, d)], r2y.at[k, d - 1], 7, r2_sem.at[1, k], at(z, y, turn(x, d)))

    def stage2(k):
        take(r2x.at[k], r2_sem.at[0, k])
        s3[k, pl.ds(0, HALF)] = s2x[k, :, :, y] + r2x[k, 0] + r2x[k, 1] + r2x[k, 2]
        take(r2y.at[k], r2_sem.at[1, k])
        s3[k, pl.ds(HALF, HALF)] = s2y[k, :, :, x] + r2y[k, 0] + r2y[k, 1] + r2y[k, 2]
        for d in range(1, RING):
            send(s3.at[k, turn(z, d)], r3.at[k, d - 1], 8, r3_sem.at[k], at(turn(z, d), y, x))

    def stage3(k):
        cols = pl.ds(pl.multiple_of(k * CW, CW), CW)
        take(r3.at[k], r3_sem.at[k])
        sums = (s3[k, z] + r3[k, 0] + r3[k, 1] + r3[k, 2]) * (1.0 / (batches * tokens))
        mean_ref[:, cols] = sums[1] * (1.0 / (RING * RING * RING))
        merged_ref[:, cols] = (sums[0] / (sums[1] + EPSILON)).astype(jnp.bfloat16)

    def step(i, c):
        @pl.when(i < blocks)
        def _():
            relay(i)

        @pl.when(i == LAG1)
        def _():
            take(rwx, rw.at[0])
            take(rwy, rw.at[1])

        @pl.when(jnp.logical_and(i >= LAG1, i < blocks + LAG1))
        def _():
            stage1(i - LAG1)

        @pl.when(jnp.logical_and(i >= LAG2, i < blocks + LAG2))
        def _():
            stage2(i - LAG2)

        @pl.when(i >= LAG3)
        def _():
            stage3(i - LAG3)

        @pl.when(i < blocks)
        def _():
            compute(i)

        return c

    lax.fori_loop(0, blocks + LAG3, step, 0)

    own = g.at[:, :, own_rows, :]
    for slot in range(3):
        take(own, send_sem.at[slot])
    take(rwx, send_sem.at[3])
    take(rwy, send_sem.at[3])
    for slot, ref in ((4, r1x), (5, r1y), (6, r2x), (7, r2y), (8, r3)):
        take(ref, send_sem.at[slot])


def local(layer_inputs, output_grads, value_weights):
    _, batches, tokens, _, features = layer_inputs.shape
    own_tokens, columns = output_grads.shape[2:]
    blocks = columns // CW
    f32, bf16 = jnp.float32, jnp.bfloat16
    dma = pltpu.SemaphoreType.DMA
    vmem = pltpu.VMEM
    merged, mean = pl.pallas_call(
        kernel,
        out_shape=(jax.ShapeDtypeStruct((ROWS, columns), bf16), jax.ShapeDtypeStruct((ROWS, columns), f32)),
        in_specs=[pl.BlockSpec(memory_space=pl.ANY)] * 3,
        out_specs=(pl.BlockSpec(memory_space=pltpu.VMEM),) * 2,
        scratch_shapes=[
            vmem((batches, tokens, features), bf16),
            vmem((batches, features, tokens), bf16),
            vmem((blocks, batches, tokens, CW), bf16),
            vmem((RING, RING, RING, ROWS, columns), bf16),
            vmem((blocks, RING, RING, RING, ROWS, CW), f32),
            vmem((RING - 1, HALF, RING, ROWS, columns), bf16),
            vmem((RING - 1, HALF, RING, ROWS, columns), bf16),
            vmem((blocks, RING - 1, HALF, RING, ROWS, CW), f32),
            vmem((blocks, RING - 1, HALF, RING, ROWS, CW), f32),
            vmem((blocks, HALF, 2, RING, ROWS, CW), f32),
            vmem((blocks, HALF, 2, RING, ROWS, CW), f32),
            vmem((blocks, RING - 1, HALF, 2, ROWS, CW), f32),
            vmem((blocks, RING - 1, HALF, 2, ROWS, CW), f32),
            vmem((blocks, RING, 2, ROWS, CW), f32),
            vmem((blocks, RING - 1, 2, ROWS, CW), f32),
            dma((batches,)), dma((blocks,)), dma, dma((9,)),
            dma((blocks,)), dma((blocks,)), dma((blocks,)), dma((2,)),
            dma((2, blocks)), dma((2, blocks)), dma((blocks,)),
        ],
        compiler_params=pltpu.CompilerParams(
            collective_id=0, has_side_effects=True, vmem_limit_bytes=56 << 20
        ),
        cost_estimate=pl.CostEstimate(
            flops=2 * batches * tokens * features * columns, bytes_accessed=10 << 20, transcendentals=0
        ),
        name="fisher_merge",
    )(
        layer_inputs.reshape(batches, tokens, features),
        output_grads.reshape(batches, own_tokens, columns),
        value_weights.reshape(RING, RING, RING, ROWS, columns),
    )
    return merged[None], mean[None]


def solution(mesh):
    return jax.shard_map(
        local,
        mesh=mesh,
        in_specs=(
            P("copy", None, None, "tp", None),
            P("copy", None, "tp", None),
            P("copy", "tp", None, None),
        ),
        out_specs=(P("tp", "copy", None), P("tp", "copy", None)),
        check_vma=False,
    )
```

time: 967 us -> 82.9 us (0.09)
  the two profiles are of different devices: /device:TPU:0 before, /device:TPU:1 now
where the time goes in v1:
time: 82.9 us; the launch traced here: 82.7 us
  Pallas kernels  79.3 us (96%)
  local copies, waits for them, and re-layouts  2.85 us (3%)
    pallas_call x1, Pallas kernels, local(): pl.pallas_call(kernel, out_shape=(jax.ShapeDtypeStruct((ROWS, columns), b...  79.3 us
    unnamed x2, local copies, waits for them, and re-layouts  2.85 us

profile of v1, /device:TPU:1, one launch (start us, length us, event | category | flops | bytes accessed | tf_op | source)
XLA Modules:
  0.0 82.7 jit_solution(670144637260469481)
XLA Ops:
  0.6 79.3 %fisher_merge.1 = (bf16[16,1024]{1,0:T(8,128)(2,1)}, f32[16,1024]{1,0:T(8,128)}) custom-call(bf16[6,512,1024]{2,1,0:T(8,128)(2,1)} %bitcast.7, bf16[6,128,1024]{2,1,0:T(8,128)(2,1)} %bitcast.9, bf16[4,4,4,16,1024]{4,3,2,1,0:T(8,128)(2,1)} %bitcast.8), custom_call_target="tpu_custom_call" | custom-call | flops 6442450944 | bytes 10485760 | tf_op jit(solution)/shard_map/fisher_merge/pallas_call | solution.py:198
  79.9 1.4 %copy.7 = bf16[1,16,1024]{2,1,0:T(8,128)(2,1)} copy(bf16[1,16,1024]{2,1,0:T(8,128)(2,1)} %bitcast.6) | data formatting | bytes 65536
  81.3 1.5 %copy.8 = f32[1,16,1024]{2,1,0:T(8,128)} copy(f32[1,16,1024]{2,1,0:T(8,128)} %bitcast.5) | data formatting | bytes 131072

commit v2 on v1

--- a/solution.py
+++ b/solution.py
@@ -10,11 +10,11 @@
 HALF = RING // 2
 ROWS = 16
 CW = 128
-LAG1, LAG2, LAG3 = 2, 3, 4
+LAG1, LAG2, LAG3 = 3, 5, 10
 MESH = pl.DeviceIdType.MESH
 
 
-def kernel(x_hbm, g_hbm, w_hbm, merged_ref, mean_ref,
+def kernel(x_hbm, g_hbm, w_hbm, out_ref,
            xv, xt, g, wv, f, rwx, rwy, r1x, r1y, s2x, s2y, r2x, r2y, s3, r3,
            x_sem, g_sem, w_sem, send_sem, rz, rc, rr, rw, r1_sem, r2_sem, r3_sem):
     batches, tokens, features = x_hbm.shape
@@ -34,6 +34,13 @@
     sibling = (copy, chip * 2 + 1 - core)
     own_rows = pl.ds(pl.multiple_of(tp * own_tokens, own_tokens), own_tokens)
     pair_rows = pl.ds(pl.multiple_of(pair[1] * own_tokens, own_tokens), own_tokens)
+
+    barrier = pltpu.get_barrier_semaphore()
+    partners = [pair, sibling]
+    for d in range(1, RING):
+        partners += [at(z, y, turn(x, d)), at(z, turn(y, d), x), at(turn(z, d), y, x)]
+    for partner in partners:
+        pl.semaphore_signal(barrier, 1, device_id=partner, device_id_type=MESH)
 
     loads = []
     for k in range(blocks):
@@ -47,12 +54,6 @@
     for load in x_loads:
         load.start()
 
-    barrier = pltpu.get_barrier_semaphore()
-    partners = [pair, sibling]
-    for d in range(1, RING):
-        partners += [at(z, y, turn(x, d)), at(z, turn(y, d), x), at(turn(z, d), y, x)]
-    for partner in partners:
-        pl.semaphore_signal(barrier, 1, device_id=partner, device_id_type=MESH)
     pl.semaphore_wait(barrier, len(partners))
 
     def send(src, dst, slot, recv, to):
@@ -91,21 +92,20 @@
         take(got, rc.at[k])
         take(got, rr.at[k])
 
-        def tile(i, c):
-            rows = pl.ds(pl.multiple_of(i * 256, 256), 256)
+        def tile(i):
+            rows = pl.ds(i * 512, 512)
             total = None
             for m in range(batches):
                 gradient = jnp.dot(xt[m, rows, :], g[k, m], preferred_element_type=jnp.float32)
                 square = gradient * gradient
                 total = square if total is None else total + square
-            f[k, i] = total.reshape(RING, RING, ROWS, CW)
-            return c
-
-        lax.fori_loop(0, HALF, tile, 0)
+            f[k, pl.ds(i * HALF, HALF)] = total.reshape(HALF, RING, RING, ROWS, CW)
+
+        tile(0)
         for d in range(1, RING):
             send(f.at[k, pl.ds(0, HALF), :, turn(x, d)], r1x.at[k, d - 1], 4, r1_sem.at[0, k],
                  at(z, y, turn(x, d)))
-        lax.fori_loop(HALF, RING, tile, 0)
+        tile(1)
         for d in range(1, RING):
             send(f.at[k, pl.ds(HALF, HALF), turn(y, d)], r1y.at[k, d - 1], 5, r1_sem.at[1, k],
                  at(z, turn(y, d), x))
@@ -139,6 +139,8 @@
         s3[k, pl.ds(0, HALF)] = s2x[k, :, :, y] + r2x[k, 0] + r2x[k, 1] + r2x[k, 2]
         take(r2y.at[k], r2_sem.at[1, k])
         s3[k, pl.ds(HALF, HALF)] = s2y[k, :, :, x] + r2y[k, 0] + r2y[k, 1] + r2y[k, 2]
+
+    def send3(k):
         for d in range(1, RING):
             send(s3.at[k, turn(z, d)], r3.at[k, d - 1], 8, r3_sem.at[k], at(turn(z, d), y, x))
 
@@ -146,8 +148,7 @@
         cols = pl.ds(pl.multiple_of(k * CW, CW), CW)
         take(r3.at[k], r3_sem.at[k])
         sums = (s3[k, z] + r3[k, 0] + r3[k, 1] + r3[k, 2]) * (1.0 / (batches * tokens))
-        mean_ref[:, cols] = sums[1] * (1.0 / (RING * RING * RING))
-        merged_ref[:, cols] = (sums[0] / (sums[1] + EPSILON)).astype(jnp.bfloat16)
+        out_ref[:, :, cols] = sums
 
     def step(i, c):
         @pl.when(i < blocks)
@@ -166,6 +167,14 @@
         @pl.when(jnp.logical_and(i >= LAG2, i < blocks + LAG2))
         def _():
             stage2(i - LAG2)
+
+        @pl.when(i == blocks)
+        def _():
+            lax.fori_loop(0, blocks - LAG2 + 1, lambda k, c: (send3(k), c)[1], 0)
+
+        @pl.when(jnp.logical_and(i > blocks, i < blocks + LAG2))
+        def _():
+            send3(i - LAG2)
 
         @pl.when(i >= LAG3)
         def _():
@@ -195,11 +204,11 @@
     f32, bf16 = jnp.float32, jnp.bfloat16
     dma = pltpu.SemaphoreType.DMA
     vmem = pltpu.VMEM
-    merged, mean = pl.pallas_call(
+    sums = pl.pallas_call(
         kernel,
-        out_shape=(jax.ShapeDtypeStruct((ROWS, columns), bf16), jax.ShapeDtypeStruct((ROWS, columns), f32)),
+        out_shape=jax.ShapeDtypeStruct((2, ROWS, columns), f32),
         in_specs=[pl.BlockSpec(memory_space=pl.ANY)] * 3,
-        out_specs=(pl.BlockSpec(memory_space=pltpu.VMEM),) * 2,
+        out_specs=pl.BlockSpec(memory_space=pltpu.VMEM),
         scratch_shapes=[
             vmem((batches, tokens, features), bf16),
             vmem((batches, features, tokens), bf16),
@@ -232,7 +241,8 @@
         output_grads.reshape(batches, own_tokens, columns),
         value_weights.reshape(RING, RING, RING, ROWS, columns),
     )
-    return merged[None], mean[None]
+    weighted, total = sums[:1], sums[1:]
+    return (weighted / (total + EPSILON)).astype(bf16), total / lax.axis_size("copy")
 
 
 def solution(mesh):

time: 82.9 us -> 67 us (0.81)
  Pallas kernels: 79.3 us -> 64.7 us
  local copies, waits for them, and re-layouts: 2.85 us -> 0 us
  other arithmetic: 0 us -> 1.52 us
    pallas_call x1, Pallas kernels: 79.3 us -> 64.7 us  [local(): pl.pallas_call(kernel, out_shape=jax.ShapeDtypeStruct((2, ROWS, columns),...]
    unnamed x2 -> x0, local copies, waits for them, and re-layouts: 2.85 us -> none
    div x0 -> x1, other arithmetic: none -> 1.52 us  [local(): total / lax.axis_size('copy')]
where the time goes in v2:
time: 67 us; the launch traced here: 66.9 us
  Pallas kernels  64.7 us (97%)
  other arithmetic  1.52 us (2%)
    pallas_call x1, Pallas kernels, local(): pl.pallas_call(kernel, out_shape=jax.ShapeDtypeStruct((2, ROWS, columns),...  64.7 us
    div x1, other arithmetic, local(): total / lax.axis_size('copy')  1.52 us

profile of v2, /device:TPU:1, one launch (start us, length us, event | category | flops | bytes accessed | tf_op | source)
XLA Modules:
  0.0 66.9 jit_solution(2043970886280418175)
XLA Ops:
  0.6 64.7 %fisher_merge.1 = f32[2,16,1024]{2,1,0:T(8,128)} custom-call(bf16[6,512,1024]{2,1,0:T(8,128)(2,1)} %bitcast.3, bf16[6,128,1024]{2,1,0:T(8,128)(2,1)} %bitcast.5, bf16[4,4,4,16,1024]{4,3,2,1,0:T(8,128)(2,1)} %bitcast.4), custom_call_target="tpu_custom_call" | custom-call | flops 6442450944 | bytes 10485760 | tf_op jit(solution)/shard_map/fisher_merge/pallas_call | solution.py:207
  65.4 1.5 %slice_multiply_fusion = (f32[1,16,1024]{2,1,0:T(8,128)}, bf16[1,16,1024]{2,1,0:T(8,128)(2,1)}) fusion(f32[2,16,1024]{2,1,0:T(8,128)} %fisher_merge.1), kind=kLoop, calls=%fused_computation.1 | loop fusion | flops 65536 | bytes 229376 | tf_op jit(solution)/shard_map/div | solution.py:245

commit v3 on v2

--- a/solution.py
+++ b/solution.py
@@ -14,8 +14,24 @@
 MESH = pl.DeviceIdType.MESH
 
 
+def spacing(high):
+    return (high * (1.0 + 1.01 / 256)).astype(jnp.bfloat16).astype(jnp.float32) - high
+
+
+def split(value):
+    high = value.astype(jnp.bfloat16)
+    near = high.astype(jnp.float32)
+    part = (value - near) * pl.reciprocal(jnp.maximum(spacing(near), 1e-30), approx=True)
+    return high, jnp.clip(jnp.floor(part * 16.0 + 8.0), 0.0, 15.0)
+
+
+def joined(high, sixteenths):
+    near = high.astype(jnp.float32)
+    return near + (sixteenths - 7.5) * (spacing(near) * (1.0 / 16))
+
+
 def kernel(x_hbm, g_hbm, w_hbm, out_ref,
-           xv, xt, g, wv, f, rwx, rwy, r1x, r1y, s2x, s2y, r2x, r2y, s3, r3,
+           xv, xt, g, wv, f, e, rwx, rwy, r1x, r1y, s2x, s2y, r2x, r2y, s3, r3,
            x_sem, g_sem, w_sem, send_sem, rz, rc, rr, rw, r1_sem, r2_sem, r3_sem):
     batches, tokens, features = x_hbm.shape
     own_tokens = g_hbm.shape[1]
@@ -37,7 +53,7 @@
 
     barrier = pltpu.get_barrier_semaphore()
     partners = [pair, sibling]
-    for d in range(1, RING):
+    for d in (2, 1, 3):
         partners += [at(z, y, turn(x, d)), at(z, turn(y, d), x), at(turn(z, d), y, x)]
     for partner in partners:
         pl.semaphore_signal(barrier, 1, device_id=partner, device_id_type=MESH)
@@ -48,12 +64,8 @@
             g_hbm.at[:, :, pl.ds(k * CW, CW)], g.at[k, :, own_rows, :], g_sem.at[k]))
     w_load = pltpu.make_async_copy(w_hbm, wv, w_sem)
     x_loads = [pltpu.make_async_copy(x_hbm.at[m], xv.at[m], x_sem.at[m]) for m in range(batches)]
-    for load in loads:
+    for load in loads + [w_load] + x_loads:
         load.start()
-    w_load.start()
-    for load in x_loads:
-        load.start()
-
     pl.semaphore_wait(barrier, len(partners))
 
     def send(src, dst, slot, recv, to):
@@ -68,7 +80,7 @@
         send(own, own, 0, rz.at[k], pair)
         send(own, own, 1, rc.at[k], sibling)
     w_load.wait()
-    for d in range(1, RING):
+    for d in (2, 1, 3):
         send(wv.at[pl.ds(0, HALF), :, turn(x, d)], rwx.at[d - 1], 3, rw.at[0], at(z, y, turn(x, d)))
         send(wv.at[pl.ds(HALF, HALF), turn(y, d)], rwy.at[d - 1], 3, rw.at[1], at(z, turn(y, d), x))
 
@@ -99,15 +111,21 @@
                 gradient = jnp.dot(xt[m, rows, :], g[k, m], preferred_element_type=jnp.float32)
                 square = gradient * gradient
                 total = square if total is None else total + square
-            f[k, pl.ds(i * HALF, HALF)] = total.reshape(HALF, RING, RING, ROWS, CW)
+            total = total.reshape(HALF, RING, RING, ROWS, CW)
+            f[k, pl.ds(i * HALF, HALF)] = total
+            high0, part0 = split(total[0])
+            high1, part1 = split(total[1])
+            e[k, i, 0] = high0
+            e[k, i, 1] = high1
+            e[k, i, 2] = (part0 * 16.0 + part1).astype(jnp.bfloat16)
 
         tile(0)
-        for d in range(1, RING):
-            send(f.at[k, pl.ds(0, HALF), :, turn(x, d)], r1x.at[k, d - 1], 4, r1_sem.at[0, k],
+        for d in (2, 1, 3):
+            send(e.at[k, 0, :, :, turn(x, d)], r1x.at[k, d - 1], 4, r1_sem.at[0, k],
                  at(z, y, turn(x, d)))
         tile(1)
-        for d in range(1, RING):
-            send(f.at[k, pl.ds(HALF, HALF), turn(y, d)], r1y.at[k, d - 1], 5, r1_sem.at[1, k],
+        for d in (2, 1, 3):
+            send(e.at[k, 1, :, turn(y, d)], r1y.at[k, d - 1], 5, r1_sem.at[1, k],
                  at(z, turn(y, d), x))
 
     def stage1(k):
@@ -117,21 +135,24 @@
             fisher = own_f
             weighted = own_f * own_w.astype(jnp.float32)
             for d in range(RING - 1):
-                fisher = fisher + rf[k, d]
-                weighted = weighted + rf[k, d] * rw_[d, :, :, :, cols].astype(jnp.float32)
+                parts = rf[k, d, 2].astype(jnp.float32)
+                part0 = jnp.floor(parts * (1.0 / 16))
+                theirs = jnp.stack([joined(rf[k, d, 0], part0), joined(rf[k, d, 1], parts - 16.0 * part0)])
+                fisher = fisher + theirs
+                weighted = weighted + theirs * rw_[d, :, :, :, cols].astype(jnp.float32)
             return weighted, fisher
 
         take(r1x.at[k], r1_sem.at[0, k])
         weighted, fisher = add(f[k, pl.ds(0, HALF), :, x], wv[pl.ds(0, HALF), :, x, :, cols], r1x, rwx)
         s2x[k, :, 0] = weighted
         s2x[k, :, 1] = fisher
-        for d in range(1, RING):
+        for d in (2, 1, 3):
             send(s2x.at[k, :, :, turn(y, d)], r2x.at[k, d - 1], 6, r2_sem.at[0, k], at(z, turn(y, d), x))
         take(r1y.at[k], r1_sem.at[1, k])
         weighted, fisher = add(f[k, pl.ds(HALF, HALF), y], wv[pl.ds(HALF, HALF), y, :, :, cols], r1y, rwy)
         s2y[k, :, 0] = weighted
         s2y[k, :, 1] = fisher
-        for d in range(1, RING):
+        for d in (2, 1, 3):
             send(s2y.at[k, :, :, turn(x, d)], r2y.at[k, d - 1], 7, r2_sem.at[1, k], at(z, y, turn(x, d)))
 
     def stage2(k):
@@ -141,7 +162,7 @@
         s3[k, pl.ds(HALF, HALF)] = s2y[k, :, :, x] + r2y[k, 0] + r2y[k, 1] + r2y[k, 2]
 
     def send3(k):
-        for d in range(1, RING):
+        for d in (2, 1, 3):
             send(s3.at[k, turn(z, d)], r3.at[k, d - 1], 8, r3_sem.at[k], at(turn(z, d), y, x))
 
     def stage3(k):
@@ -215,10 +236,11 @@
             vmem((blocks, batches, tokens, CW), bf16),
             vmem((RING, RING, RING, ROWS, columns), bf16),
             vmem((blocks, RING, RING, RING, ROWS, CW), f32),
+            vmem((blocks, HALF, 3, RING, RING, ROWS, CW), bf16),
             vmem((RING - 1, HALF, RING, ROWS, columns), bf16),
             vmem((RING - 1, HALF, RING, ROWS, columns), bf16),
-            vmem((blocks, RING - 1, HALF, RING, ROWS, CW), f32),
-            vmem((blocks, RING - 1, HALF, RING, ROWS, CW), f32),
+            vmem((blocks, RING - 1, 3, RING, ROWS, CW), bf16),
+            vmem((blocks, RING - 1, 3, RING, ROWS, CW), bf16),
             vmem((blocks, HALF, 2, RING, ROWS, CW), f32),
             vmem((blocks, HALF, 2, RING, ROWS, CW), f32),
             vmem((blocks, RING - 1, HALF, 2, ROWS, CW), f32),

time: 67 us -> 65 us (0.970)
  Pallas kernels: 64.7 us -> 62.7 us
    pallas_call x1, Pallas kernels: 64.7 us -> 62.7 us  [local(): pl.pallas_call(kernel, out_shape=jax.ShapeDtypeStruct((2, ROWS, columns),...]
where the time goes in v3:
time: 65 us; the launch traced here: 64.8 us
  Pallas kernels  62.7 us (96%)
  other arithmetic  1.52 us (2%)
    pallas_call x1, Pallas kernels, local(): pl.pallas_call(kernel, out_shape=jax.ShapeDtypeStruct((2, ROWS, columns),...  62.7 us
    div x1, other arithmetic, local(): total / lax.axis_size('copy')  1.52 us

profile of v3, /device:TPU:1, one launch (start us, length us, event | category | flops | bytes accessed | tf_op | source)
XLA Modules:
  0.0 64.8 jit_solution(112182781458167241)
XLA Ops:
  0.6 62.7 %fisher_merge.1 = f32[2,16,1024]{2,1,0:T(8,128)} custom-call(bf16[6,512,1024]{2,1,0:T(8,128)(2,1)} %bitcast.3, bf16[6,128,1024]{2,1,0:T(8,128)(2,1)} %bitcast.5, bf16[4,4,4,16,1024]{4,3,2,1,0:T(8,128)(2,1)} %bitcast.4), custom_call_target="tpu_custom_call" | custom-call | flops 6442450944 | bytes 10485760 | tf_op jit(solution)/shard_map/fisher_merge/pallas_call | solution.py:228
  63.3 1.5 %slice_multiply_fusion = (f32[1,16,1024]{2,1,0:T(8,128)}, bf16[1,16,1024]{2,1,0:T(8,128)(2,1)}) fusion(f32[2,16,1024]{2,1,0:T(8,128)} %fisher_merge.1), kind=kLoop, calls=%fused_computation.1 | loop fusion | flops 65536 | bytes 229376 | tf_op jit(solution)/shard_map/div | solution.py:267

commit v4 on v3

--- a/solution.py
+++ b/solution.py
@@ -115,17 +115,18 @@
             f[k, pl.ds(i * HALF, HALF)] = total
             high0, part0 = split(total[0])
             high1, part1 = split(total[1])
-            e[k, i, 0] = high0
-            e[k, i, 1] = high1
-            e[k, i, 2] = (part0 * 16.0 + part1).astype(jnp.bfloat16)
+            parts = (part0 * 16.0 + part1).astype(jnp.bfloat16)
+            for to in range(RING):
+                for kind, value in enumerate((high0, high1, parts)):
+                    e[k, i, to, kind] = value[:, to] if i == 0 else value[to]
 
         tile(0)
         for d in (2, 1, 3):
-            send(e.at[k, 0, :, :, turn(x, d)], r1x.at[k, d - 1], 4, r1_sem.at[0, k],
+            send(e.at[k, 0, turn(x, d)], r1x.at[k, d - 1], 4, r1_sem.at[0, k],
                  at(z, y, turn(x, d)))
         tile(1)
         for d in (2, 1, 3):
-            send(e.at[k, 1, :, turn(y, d)], r1y.at[k, d - 1], 5, r1_sem.at[1, k],
+            send(e.at[k, 1, turn(y, d)], r1y.at[k, d - 1], 5, r1_sem.at[1, k],
                  at(z, turn(y, d), x))
 
     def stage1(k):
@@ -144,22 +145,24 @@
 
         take(r1x.at[k], r1_sem.at[0, k])
         weighted, fisher = add(f[k, pl.ds(0, HALF), :, x], wv[pl.ds(0, HALF), :, x, :, cols], r1x, rwx)
-        s2x[k, :, 0] = weighted
-        s2x[k, :, 1] = fisher
-        for d in (2, 1, 3):
-            send(s2x.at[k, :, :, turn(y, d)], r2x.at[k, d - 1], 6, r2_sem.at[0, k], at(z, turn(y, d), x))
+        for to in range(RING):
+            s2x[k, to, :, 0] = weighted[:, to]
+            s2x[k, to, :, 1] = fisher[:, to]
+        for d in (2, 1, 3):
+            send(s2x.at[k, turn(y, d)], r2x.at[k, d - 1], 6, r2_sem.at[0, k], at(z, turn(y, d), x))
         take(r1y.at[k], r1_sem.at[1, k])
         weighted, fisher = add(f[k, pl.ds(HALF, HALF), y], wv[pl.ds(HALF, HALF), y, :, :, cols], r1y, rwy)
-        s2y[k, :, 0] = weighted
-        s2y[k, :, 1] = fisher
-        for d in (2, 1, 3):
-            send(s2y.at[k, :, :, turn(x, d)], r2y.at[k, d - 1], 7, r2_sem.at[1, k], at(z, y, turn(x, d)))
+        for to in range(RING):
+            s2y[k, to, :, 0] = weighted[:, to]
+            s2y[k, to, :, 1] = fisher[:, to]
+        for d in (2, 1, 3):
+            send(s2y.at[k, turn(x, d)], r2y.at[k, d - 1], 7, r2_sem.at[1, k], at(z, y, turn(x, d)))
 
     def stage2(k):
         take(r2x.at[k], r2_sem.at[0, k])
-        s3[k, pl.ds(0, HALF)] = s2x[k, :, :, y] + r2x[k, 0] + r2x[k, 1] + r2x[k, 2]
+        s3[k, pl.ds(0, HALF)] = s2x[k, y] + r2x[k, 0] + r2x[k, 1] + r2x[k, 2]
         take(r2y.at[k], r2_sem.at[1, k])
-        s3[k, pl.ds(HALF, HALF)] = s2y[k, :, :, x] + r2y[k, 0] + r2y[k, 1] + r2y[k, 2]
+        s3[k, pl.ds(HALF, HALF)] = s2y[k, x] + r2y[k, 0] + r2y[k, 1] + r2y[k, 2]
 
     def send3(k):
         for d in (2, 1, 3):
@@ -236,13 +239,13 @@
             vmem((blocks, batches, tokens, CW), bf16),
             vmem((RING, RING, RING, ROWS, columns), bf16),
             vmem((blocks, RING, RING, RING, ROWS, CW), f32),
-            vmem((blocks, HALF, 3, RING, RING, ROWS, CW), bf16),
+            vmem((blocks, HALF, RING, 3, RING, ROWS, CW), bf16),
             vmem((RING - 1, HALF, RING, ROWS, columns), bf16),
             vmem((RING - 1, HALF, RING, ROWS, columns), bf16),
             vmem((blocks, RING - 1, 3, RING, ROWS, CW), bf16),
             vmem((blocks, RING - 1, 3, RING, ROWS, CW), bf16),
-            vmem((blocks, HALF, 2, RING, ROWS, CW), f32),
-            vmem((blocks, HALF, 2, RING, ROWS, CW), f32),
+            vmem((blocks, RING, HALF, 2, ROWS, CW), f32),
+            vmem((blocks, RING, HALF, 2, ROWS, CW), f32),
             vmem((blocks, RING - 1, HALF, 2, ROWS, CW), f32),
             vmem((blocks, RING - 1, HALF, 2, ROWS, CW), f32),
             vmem((blocks, RING, 2, ROWS, CW), f32),

time: 65 us -> 64.7 us (level)
  no operation moved by 1% of the time
where the time goes in v4:
time: 64.7 us; the launch traced here: 64.6 us
  Pallas kernels  62.4 us (96%)
  other arithmetic  1.52 us (2%)
    pallas_call x1, Pallas kernels, local(): pl.pallas_call(kernel, out_shape=jax.ShapeDtypeStruct((2, ROWS, columns),...  62.4 us
    div x1, other arithmetic, local(): total / lax.axis_size('copy')  1.52 us

profile of v4, /device:TPU:1, one launch (start us, length us, event | category | flops | bytes accessed | tf_op | source)
XLA Modules:
  0.0 64.6 jit_solution(9915759923183648083)
XLA Ops:
  0.6 62.4 %fisher_merge.1 = f32[2,16,1024]{2,1,0:T(8,128)} custom-call(bf16[6,512,1024]{2,1,0:T(8,128)(2,1)} %bitcast.3, bf16[6,128,1024]{2,1,0:T(8,128)(2,1)} %bitcast.5, bf16[4,4,4,16,1024]{4,3,2,1,0:T(8,128)(2,1)} %bitcast.4), custom_call_target="tpu_custom_call" | custom-call | flops 6442450944 | bytes 10485760 | tf_op jit(solution)/shard_map/fisher_merge/pallas_call | solution.py:231
  63.0 1.5 %slice_multiply_fusion = (f32[1,16,1024]{2,1,0:T(8,128)}, bf16[1,16,1024]{2,1,0:T(8,128)(2,1)}) fusion(f32[2,16,1024]{2,1,0:T(8,128)} %fisher_merge.1), kind=kLoop, calls=%fused_computation.1 | loop fusion | flops 65536 | bytes 229376 | tf_op jit(solution)/shard_map/div | solution.py:270

commit v5 on v4

--- a/solution.py
+++ b/solution.py
@@ -21,7 +21,7 @@
 def split(value):
     high = value.astype(jnp.bfloat16)
     near = high.astype(jnp.float32)
-    part = (value - near) * pl.reciprocal(jnp.maximum(spacing(near), 1e-30), approx=True)
+    part = (value - near) * pl.reciprocal(jnp.maximum(spacing(near), 1e-37), approx=True)
     return high, jnp.clip(jnp.floor(part * 16.0 + 8.0), 0.0, 15.0)
 
 

time: 64.7 us -> 64.7 us (level)
  no operation moved by 1% of the time
where the time goes in v5:
time: 64.7 us; the launch traced here: 64.6 us
  Pallas kernels  62.4 us (96%)
  other arithmetic  1.52 us (2%)
    pallas_call x1, Pallas kernels, local(): pl.pallas_call(kernel, out_shape=jax.ShapeDtypeStruct((2, ROWS, columns),...  62.4 us
    div x1, other arithmetic, local(): total / lax.axis_size('copy')  1.52 us

profile of v5, /device:TPU:1, one launch (start us, length us, event | category | flops | bytes accessed | tf_op | source)
XLA Modules:
  0.0 64.6 jit_solution(8577573432704521895)
XLA Ops:
  0.6 62.4 %fisher_merge.1 = f32[2,16,1024]{2,1,0:T(8,128)} custom-call(bf16[6,512,1024]{2,1,0:T(8,128)(2,1)} %bitcast.3, bf16[6,128,1024]{2,1,0:T(8,128)(2,1)} %bitcast.5, bf16[4,4,4,16,1024]{4,3,2,1,0:T(8,128)(2,1)} %bitcast.4), custom_call_target="tpu_custom_call" | custom-call | flops 6442450944 | bytes 10485760 | tf_op jit(solution)/shard_map/fisher_merge/pallas_call | solution.py:231
  63.0 1.5 %slice_multiply_fusion = (f32[1,16,1024]{2,1,0:T(8,128)}, bf16[1,16,1024]{2,1,0:T(8,128)(2,1)}) fusion(f32[2,16,1024]{2,1,0:T(8,128)} %fisher_merge.1), kind=kLoop, calls=%fused_computation.1 | loop fusion | flops 65536 | bytes 229376 | tf_op jit(solution)/shard_map/div | solution.py:270
